TPU v7x, 32 devices: a whole 2x2x4 slice. The times are simulated.
32 devices in a mesh: ctx: 16 (over z, x, core), kvh: 2 (over y).
Axes of the slice: x: 2, y: 2, z: 4, core: 2. Of those that a mesh axis runs over, the one named last changes fastest.
Arguments:
- queries: bfloat16 [8192, 3584], P('ctx', 'kvh'), may hold values from -7.5 to 7.5
- keys: bfloat16 [8192, 512], P('ctx', 'kvh'), may hold values from -6 to 6
- values: bfloat16 [8192, 512], P('ctx', 'kvh'), may hold values from -6 to 6
- columns: int32 [28, 16], P('kvh'), may hold values from 0 to 63, as said below
- offsets: int32 [28, 128], P('kvh'), may hold values from 0 to 511, as said below
- out_weight: bfloat16 [3584, 3584], P('kvh'), may hold values from -0.09375 to 0.09375
Outputs:
- mixed: bfloat16 [8192, 3584], P('ctx', 'kvh')
Inputs may be any that keep to these rules, and one draw needn't show every extreme that they name: `columns`: each row lists 16 different blocks of 128 tokens. Rows h with equal h // 7 share a KV head; the union of their lists holds at most 2 blocks among the tokens of any one aligned run of 512 tokens, and exactly 2 among tokens 0 to 511. `offsets`: each row holds 128 different diagonal distances, 0 and 1 among them.
All inputs are finite; a program needn't handle non-finite values.
Results may differ from a plain program's by a relative error of at most 0.012.
Values may be sent and summed in bfloat16 or wider, within the bound.
A program may use at most 320 MiB of HBM per device.

v0:
```python
import functools
import math

import jax
import jax.numpy as jnp
from jax import lax
from jax.experimental import pallas as pl
from jax.experimental.pallas import tpu as pltpu
from jax.sharding import PartitionSpec as P

HD = 128
BLK = 128
NV = 16
CAP = 2
WIN = 512
WB = WIN // BLK
NEAR = WIN + BLK
PARTS = 2
PAIR = 2
EXP2_SCALE = math.log2(math.e) / math.sqrt(HD)

masked_score = -1e30


def shifted(value, axis, by):
    devices = lax.axis_size(axis)
    pairs = [(i, i + by) for i in range(devices) if 0 <= i + by < devices]
    return lax.ppermute(value, axis, pairs)


def pack_kernel(picked_ref, key_ref, value_ref, out_ref):
    out_ref[0, :, :HD] = key_ref[...]
    out_ref[0, :, HD:] = value_ref[...]


def pack_blocks(keys, values, picked, kv_heads):
    def source(kv, slot, picked_ref):
        return picked_ref[kv * CAP + slot], kv

    return pl.pallas_call(
        pack_kernel,
        grid_spec=pltpu.PrefetchScalarGridSpec(
            num_scalar_prefetch=1,
            grid=(kv_heads, CAP),
            in_specs=[pl.BlockSpec((BLK, HD), source), pl.BlockSpec((BLK, HD), source)],
            out_specs=pl.BlockSpec((1, BLK, 2 * HD), lambda kv, slot, _: (kv, slot, 0)),
        ),
        out_shape=jax.ShapeDtypeStruct((kv_heads, CAP * BLK, 2 * HD), keys.dtype),
    )(picked.reshape(-1), keys, values)


def attend_kernel(
    part, chunks, group_size,
    columns_ref, rank_ref, query_ref, band_ref, pool_ref,
    earlier_keys_ref, keys_ref, earlier_values_ref, values_ref,
    out_ref,
    window_k, window_v, far_k, far_v, far_s, near_s, far_p, near_p,
):
    step = pl.program_id(0)
    shard = lax.axis_index("ctx")
    kv_heads = window_k.shape[0]
    block_count = pool_ref.shape[0] * WB
    first = part * chunks

    @pl.when(step == 0)
    def _():
        ones = jnp.ones((2 * WIN, HD), jnp.bfloat16)
        for kv in range(kv_heads):
            lanes = slice(kv * HD, (kv + 1) * HD)
            window_k[kv, :WIN] = earlier_keys_ref[:, lanes]
            window_k[kv, WIN:] = keys_ref[:, lanes]
            window_v[kv, :WIN, :HD] = earlier_values_ref[:, lanes]
            window_v[kv, WIN:, :HD] = values_ref[:, lanes]
            window_v[kv, :, HD:] = ones
        for pair in range(PAIR):
            far_v[pair, :, HD:] = jnp.ones((NV * BLK, HD), jnp.bfloat16)

    before = jnp.where(shard == 0, masked_score, 0.0).astype(jnp.float32)
    row_lane = lax.broadcasted_iota(jnp.int32, (BLK, BLK), 0)
    key_lane = lax.broadcasted_iota(jnp.int32, (BLK, BLK), 1)
    lower = row_lane >= key_lane

    tops = []
    for pair in range(PAIR):
        head = step * PAIR + pair
        kv = head // group_size
        query = query_ref[:, pair * HD : (pair + 1) * HD]
        blocks = []
        for n in range(NV):
            block = columns_ref[head * NV + n]
            blocks.append(block)
            rank = rank_ref[kv * block_count + block]
            rows = pl.ds(pl.multiple_of(rank * BLK, BLK), BLK)
            far_k[pair, n * BLK : (n + 1) * BLK] = pool_ref[block // WB, kv, rows, :HD]
            far_v[pair, n * BLK : (n + 1) * BLK, :HD] = pool_ref[block // WB, kv, rows, HD:]
        band = pltpu.roll(
            jnp.broadcast_to(band_ref[pair], (BLK, NEAR + BLK)), 0, 1, stride=1, stride_axis=0
        )[:, :NEAR]
        peak = [None] * chunks
        for a in range(chunks):
            rows = slice(a * BLK, (a + 1) * BLK)
            scores = lax.dot_general(
                query[rows],
                window_k[kv, (first + a) * BLK : (first + a) * BLK + NEAR],
                (((1,), (1,)), ((), ())),
                preferred_element_type=jnp.float32,
            )
            oldest = (shard - 1) * WB + first + a
            hit = blocks[0] == oldest
            for n in range(1, NV):
                hit = hit | (blocks[n] == oldest)
            extra = jnp.where(hit, 0.0, masked_score).astype(jnp.float32)
            for t in range(WB + 1):
                lanes = slice(t * BLK, (t + 1) * BLK)
                mask = band[:, lanes]
                if t == 0:
                    mask = jnp.where(lower, extra, mask)
                if first + a + t < WB:
                    mask = mask + before
                tile = scores[:, lanes] + mask
                near_s[pair, rows, lanes] = tile
                peak[a] = tile if peak[a] is None else jnp.maximum(peak[a], tile)
        wide = 4
        for j in range(NV // wide):
            scores = lax.dot_general(
                query,
                far_k[pair, j * wide * BLK : (j + 1) * wide * BLK],
                (((1,), (1,)), ((), ())),
                preferred_element_type=jnp.float32,
            )
            for a in range(chunks):
                rows = slice(a * BLK, (a + 1) * BLK)
                for t in range(wide):
                    n = j * wide + t
                    old = blocks[n] < (shard - 1) * WB + first + a
                    bias = jnp.where(old, 0.0, masked_score).astype(jnp.float32)
                    tile = scores[rows, t * BLK : (t + 1) * BLK] + bias
                    far_s[pair, rows, n * BLK : (n + 1) * BLK] = tile
                    peak[a] = jnp.maximum(peak[a], tile)
        tops.append([jnp.max(peak[a], axis=1, keepdims=True) for a in range(chunks)])

    for pair in range(PAIR):
        head = step * PAIR + pair
        kv = head // group_size
        for a in range(chunks):
            rows = slice(a * BLK, (a + 1) * BLK)
            top = jnp.broadcast_to(tops[pair][a], (BLK, BLK))
            for t in range(WB + 1):
                lanes = slice(t * BLK, (t + 1) * BLK)
                near_p[pair, rows, lanes] = jnp.exp2(
                    (near_s[pair, rows, lanes] - top) * EXP2_SCALE
                ).astype(jnp.bfloat16)
            for n in range(NV):
                lanes = slice(n * BLK, (n + 1) * BLK)
                far_p[pair, rows, lanes] = jnp.exp2(
                    (far_s[pair, rows, lanes] - top) * EXP2_SCALE
                ).astype(jnp.bfloat16)
        total = jnp.dot(far_p[pair], far_v[pair], preferred_element_type=jnp.float32)
        for a in range(chunks):
            rows = slice(a * BLK, (a + 1) * BLK)
            sums = total[rows] + jnp.dot(
                near_p[pair, rows],
                window_v[kv, (first + a) * BLK : (first + a) * BLK + NEAR],
                preferred_element_type=jnp.float32,
            )
            out_ref[rows, pair * HD : (pair + 1) * HD] = (
                sums[:, :HD] / sums[:, HD:]
            ).astype(jnp.bfloat16)


def attend(part, queries, band, pool, columns, rank, earlier_keys, keys, earlier_values, values):
    shard_rows, width = queries.shape
    rows = shard_rows // PARTS
    chunks = rows // BLK
    local_heads = width // HD
    kv_heads = keys.shape[1] // HD
    whole = pl.BlockSpec(memory_space=pltpu.VMEM)
    return pl.pallas_call(
        functools.partial(attend_kernel, part, chunks, local_heads // kv_heads),
        grid_spec=pltpu.PrefetchScalarGridSpec(
            num_scalar_prefetch=2,
            grid=(local_heads // PAIR,),
            in_specs=[
                pl.BlockSpec((rows, PAIR * HD), lambda k, *_: (part, k)),
                pl.BlockSpec((PAIR, 1, NEAR + BLK), lambda k, *_: (k, 0, 0)),
                whole, whole, whole, whole, whole,
            ],
            out_specs=pl.BlockSpec((rows, PAIR * HD), lambda k, *_: (0, k)),
            scratch_shapes=[
                pltpu.VMEM((kv_heads, 2 * WIN, HD), jnp.bfloat16),
                pltpu.VMEM((kv_heads, 2 * WIN, 2 * HD), jnp.bfloat16),
                pltpu.VMEM((PAIR, NV * BLK, HD), jnp.bfloat16),
                pltpu.VMEM((PAIR, NV * BLK, 2 * HD), jnp.bfloat16),
                pltpu.VMEM((PAIR, rows, NV * BLK), jnp.float32),
                pltpu.VMEM((PAIR, rows, NEAR), jnp.float32),
                pltpu.VMEM((PAIR, rows, NV * BLK), jnp.bfloat16),
                pltpu.VMEM((PAIR, rows, NEAR), jnp.bfloat16),
            ],
        ),
        out_shape=jax.ShapeDtypeStruct((rows, width), jnp.bfloat16),
        compiler_params=pltpu.CompilerParams(vmem_limit_bytes=56 * 1024 * 1024),
        cost_estimate=pl.CostEstimate(
            flops=4 * rows * (NV * BLK + NEAR) * width,
            bytes_accessed=2 * pool.size + 4 * rows * width,
            transcendentals=rows * (NV * BLK + NEAR) * local_heads,
        ),
    )(columns.reshape(-1), rank.reshape(-1), queries, band, pool,
      earlier_keys, keys, earlier_values, values)


def shards(queries, keys, values, columns, offsets, out_weight):
    shard_rows = queries.shape[0]
    kv_heads = keys.shape[1] // HD
    owned = shard_rows // BLK
    shard_count = lax.axis_size("ctx")
    shard_index = lax.axis_index("ctx")
    earlier_keys, earlier_values = shifted((keys, values), "ctx", 1)

    block_lane = jnp.arange(shard_count * owned, dtype=jnp.int32)
    listed = jnp.any(
        columns.reshape(kv_heads, -1)[:, :, None] == block_lane[None, None, :], axis=1
    ).astype(jnp.int32).reshape(kv_heads, shard_count, owned)
    earlier = jnp.arange(owned)[:, None] < jnp.arange(owned)[None, :]
    rank = jnp.sum(listed[:, :, :, None] * earlier[None, None].astype(jnp.int32), axis=2)
    own_listed = lax.dynamic_index_in_dim(listed, shard_index, 1, keepdims=False)
    own_rank = lax.dynamic_index_in_dim(rank, shard_index, 1, keepdims=False)
    slot_lane = jnp.arange(CAP, dtype=jnp.int32)
    chosen = (own_listed[:, None, :] > 0) & (own_rank[:, None, :] == slot_lane[None, :, None])
    picked = jnp.sum(
        jnp.where(chosen, jnp.arange(owned, dtype=jnp.int32)[None, None, :], 0), axis=2
    )
    pool = lax.all_gather(pack_blocks(keys, values, picked, kv_heads), "ctx", axis=0)

    distance = WIN - jnp.arange(NEAR + BLK, dtype=jnp.int32)
    band = jnp.where(
        jnp.any(offsets[:, :, None] == distance[None, None, :], axis=1), 0.0, masked_score
    ).astype(jnp.float32)[:, None, :]

    half = out_weight.shape[1] // 2
    upper = lax.axis_index("kvh") == 1
    results = []
    for part in range(PARTS):
        attended = attend(
            part, queries, band, pool, columns, rank,
            earlier_keys, keys, earlier_values, values,
        )
        mixed = jnp.dot(attended, out_weight, preferred_element_type=jnp.float32)
        low, high = mixed[:, :half], mixed[:, half:]
        away = jnp.where(upper, low, high).astype(jnp.bfloat16)
        home = jnp.where(upper, high, low)
        arrived = lax.ppermute(away, "kvh", [(0, 1), (1, 0)])
        results.append((home + arrived.astype(jnp.float32)).astype(jnp.bfloat16))
    return jnp.concatenate(results, axis=0)


def solution(mesh):
    placed = (
        P("ctx", "kvh"),
        P("ctx", "kvh"),
        P("ctx", "kvh"),
        P("kvh", None),
        P("kvh", None),
        P("kvh", None),
    )
    return jax.shard_map(
        shards, mesh=mesh, in_specs=placed, out_specs=P("ctx", "kvh"), check_vma=False
    )
```

profile of v0, /device:TPU:0, one launch (start us, length us, event | category | flops | bytes accessed | tf_op | source)
XLA Modules:
  0.0 157.9 jit_solution(13408935419250727890)
XLA Ops:
  6.5 0.0 all-gather.3.cloned.1.call-start
  6.5 0.8 eq.47
  7.3 0.1 fusion
  7.4 0.1 reshape.53
  7.5 0.1 copy.12
  7.6 0.1 multiply_reduce_fusion
  7.7 0.2 dynamic-slice_reduce_fusion
  7.9 0.2 fusion.1
  8.1 0.7 reshape.52.picked_ref
  8.8 3.5 %shard_map.64 = bf16[2,256,256]{2,1,0:T(8,128)(2,1)} custom-call(s32[4]{0:T(128)} %reshape.52.picked_ref, bf16[512,256]{1,0:T(8,128)(2,1)} %keys_ref.3, bf16[512,256]{1,0:T(8,128)(2,1)} %values_ref.3), custom_call_target="tpu_custom_call" | custom-call | tf_op jit(solution)/shard_map/pallas_call | solution.py:40
  12.3 0.0 all-gather.3.cloned.1.call-update
  12.3 2.4 %collective-permute-start = (bf16[512,256]{1,0:T(8,128)(2,1)}, bf16[512,256]{1,0:T(8,128)(2,1)S(1)}, u32[]{:S(2)}, u32[]{:S(2)}) collective-permute-start(bf16[512,256]{1,0:T(8,128)(2,1)} %keys_ref.3), channel_id=1, source_target_pairs={{0,2},{2,4},{4,6},{6,8},{8,10},{10,12},{12,14},{14,16},{16,18},{18... | collective-permute-start | bytes 786440 | tf_op jit(solution)/shard_map/ppermute | solution.py:28
  14.7 4.5 %collective-permute-start.1 = (bf16[512,256]{1,0:T(8,128)(2,1)}, bf16[512,256]{1,0:T(8,128)(2,1)S(1)}, u32[]{:S(2)}, u32[]{:S(2)}) collective-permute-start(bf16[512,256]{1,0:T(8,128)(2,1)} %values_ref.3), channel_id=1, source_target_pairs={{0,2},{2,4},{4,6},{6,8},{8,10},{10,12},{12,14},{14,16},{16,18},{18... | collective-permute-start | bytes 786440 | tf_op jit(solution)/shard_map/ppermute | solution.py:28
  19.3 1.6 %compare_reduce_fusion = pred[14,768]{1,0:T(8,128)(4,1)S(1)} fusion(s32[768]{0:T(1024)S(1)} %iota_subtract_fusion, s32[14,128]{1,0:T(8,128)} %param.10), kind=kLoop, calls=%fused_computation | loop fusion | flops 2741760 | bytes 20992 | tf_op jit(solution)/shard_map/reduce_or | solution.py:236
  20.9 1.3 reshape.50.columns_ref
  22.2 0.1 copy.13
  22.3 0.7 reshape.51.rank_ref
  23.0 0.6 select_n.45.band_ref
  23.6 0.0 collective-permute-done.earlier_keys_ref
  23.6 0.0 copy-start
  23.6 0.0 collective-permute-done.1.earlier_values_ref
  23.6 0.0 copy-start.1
  23.6 42.1 %all-gather.3.cloned.1.call-done = bf16[32,256,256]{2,1,0:T(8,128)(2,1)} async-done(((bf16[2,256,256]{2,1,0:T(8,128)(2,1)}), bf16[32,256,256]{2,1,0:T(8,128)(2,1)}) %all-gather.3.cloned.1.call-update) | async-done | bytes 4194320 | tf_op jit(solution)/shard_map/all_gather | solution.py:232
  65.8 0.0 copy-done
  65.8 0.0 copy-done.1
  65.8 23.0 %shard_map.65 = bf16[256,1792]{1,0:T(8,128)(2,1)} custom-call(s32[224]{0:T(256)} %reshape.50.columns_ref, s32[128]{0:T(128)} %reshape.51.rank_ref, bf16[512,1792]{1,0:T(8,128)(2,1)} %query_ref.3, f32[14,1,768]{2,1,0:T(1,128)} %select_n.45.band_ref, bf16[16,2,256,256]{3,2,1,0:T(8,128)(2,1)} %bitcast.9, bf16[512,256]{1,0:T(8,128)(2,1)} %copy-done, ...), custom_call_target="tpu_custom_call" | custom-call | flops 4932501504 | bytes 6029312 | tf_op jit(solution)/shard_map/pallas_call | solution.py:178
  88.7 6.8 %fusion.3 = f32[256,3584]{1,0:T(8,128)S(1)} fusion(bf16[256,1792]{1,0:T(8,128)(2,1)} %shard_map.65, bf16[1792,3584]{1,0:T(8,128)(2,1)} %param.11), kind=kOutput, calls=%fused_computation.18 | convolution fusion | flops 3288334336 | bytes 17432576 | tf_op jit(solution)/shard_map/dot_general | solution.py:247
  95.5 0.2 select_convert_fusion.1
  95.7 1.5 collective-permute-start.2
  97.2 22.9 %shard_map.66 = bf16[256,1792]{1,0:T(8,128)(2,1)} custom-call(s32[224]{0:T(256)} %reshape.50.columns_ref, s32[128]{0:T(128)} %reshape.51.rank_ref, bf16[512,1792]{1,0:T(8,128)(2,1)} %query_ref.3, f32[14,1,768]{2,1,0:T(1,128)} %select_n.45.band_ref, bf16[16,2,256,256]{3,2,1,0:T(8,128)(2,1)} %bitcast.10, bf16[512,256]{1,0:T(8,128)(2,1)} %copy-done, ...), custom_call_target="tpu_custom_call" | custom-call | flops 4932501504 | bytes 6029312 | tf_op jit(solution)/shard_map/pallas_call | solution.py:178
  120.1 6.8 %fusion.4 = f32[256,3584]{1,0:T(8,128)S(1)} fusion(bf16[256,1792]{1,0:T(8,128)(2,1)} %shard_map.66, bf16[1792,3584]{1,0:T(8,128)(2,1)} %param.11), kind=kOutput, calls=%fused_computation.19 | convolution fusion | flops 3288334336 | bytes 17432576 | tf_op jit(solution)/shard_map/dot_general | solution.py:247
  126.9 0.2 select_convert_fusion
  127.0 0.6 collective-permute-start.3
  127.7 0.0 collective-permute-done.2
  127.7 0.3 add_convert_fusion.1
  127.9 21.4 %collective-permute-done.3 = bf16[256,1792]{1,0:T(8,128)(2,1)S(1)} collective-permute-done((bf16[256,1792]{1,0:T(8,128)(2,1)S(1)}, bf16[256,1792]{1,0:T(8,128)(2,1)S(1)}, u32[]{:S(2)}, u32[]{:S(2)}) %collective-permute-start.3) | collective-permute-done | bytes 917536 | tf_op jit(solution)/shard_map/ppermute | solution.py:251
  149.3 0.3 add_convert_fusion
  149.7 1.4 pad_maximum_fusion
  (6 shorter events, 0.0 us)
Async XLA Ops:
  6.5 59.2 %all-gather.3.cloned.1.call-start = ((), (), s32[]{:S(2)}) async-start(), calls=%async_computation | async-start | bytes 4456448 | tf_op jit(solution)/shard_map/all_gather | solution.py:232
  12.3 11.3 %collective-permute-start = (bf16[512,256]{1,0:T(8,128)(2,1)}, bf16[512,256]{1,0:T(8,128)(2,1)S(1)}, u32[]{:S(2)}, u32[]{:S(2)}) collective-permute-start(bf16[512,256]{1,0:T(8,128)(2,1)} %keys_ref.3), channel_id=1, source_target_pairs={{0,2},{2,4},{4,6},{6,8},{8,10},{10,12},{12,14},{14,16},{16,18},{18... | collective-permute-start | bytes 786440 | tf_op jit(solution)/shard_map/ppermute | solution.py:28
  14.7 8.9 %collective-permute-start.1 = (bf16[512,256]{1,0:T(8,128)(2,1)}, bf16[512,256]{1,0:T(8,128)(2,1)S(1)}, u32[]{:S(2)}, u32[]{:S(2)}) collective-permute-start(bf16[512,256]{1,0:T(8,128)(2,1)} %values_ref.3), channel_id=1, source_target_pairs={{0,2},{2,4},{4,6},{6,8},{8,10},{10,12},{12,14},{14,16},{16,18},{18... | collective-permute-start | bytes 786440 | tf_op jit(solution)/shard_map/ppermute | solution.py:28
  23.6 42.1 %copy-start = (bf16[512,256]{1,0:T(8,128)(2,1)}, bf16[512,256]{1,0:T(8,128)(2,1)S(1)}, u32[]{:S(2)}) copy-start(bf16[512,256]{1,0:T(8,128)(2,1)S(1)} %collective-permute-done.earlier_keys_ref) | copy-start | bytes 786436
  23.6 42.1 %copy-start.1 = (bf16[512,256]{1,0:T(8,128)(2,1)}, bf16[512,256]{1,0:T(8,128)(2,1)S(1)}, u32[]{:S(2)}) copy-start(bf16[512,256]{1,0:T(8,128)(2,1)S(1)} %collective-permute-done.1.earlier_values_ref) | copy-start | bytes 786436
  95.7 32.0 %collective-permute-start.2 = (bf16[256,1792]{1,0:T(8,128)(2,1)S(1)}, bf16[256,1792]{1,0:T(8,128)(2,1)S(1)}, u32[]{:S(2)}, u32[]{:S(2)}) collective-permute-start(bf16[256,1792]{1,0:T(8,128)(2,1)S(1)} %select_convert_fusion.1), channel_id=1, source_target_pairs={{0,1},{1,0},{2,3},{3,2},{4,5},{5,4},{6,7},{7,6},{8,9},{9,8},{10,11... | collective-permute-start | bytes 2752520 | tf_op jit(solution)/shard_map/ppermute | solution.py:251
  127.0 22.3 %collective-permute-start.3 = (bf16[256,1792]{1,0:T(8,128)(2,1)S(1)}, bf16[256,1792]{1,0:T(8,128)(2,1)S(1)}, u32[]{:S(2)}, u32[]{:S(2)}) collective-permute-start(bf16[256,1792]{1,0:T(8,128)(2,1)S(1)} %select_convert_fusion), channel_id=1, source_target_pairs={{0,1},{1,0},{2,3},{3,2},{4,5},{5,4},{6,7},{7,6},{8,9},{9,8},{10,11... | collective-permute-start | bytes 2752520 | tf_op jit(solution)/shard_map/ppermute | solution.py:251
Sparse Core Ops, SparseCore 0:
  12.5 53.2 all-gather.2
where the time goes:
time: 158 us
  waiting for transfers between devices  63.5 us (40%)
  Pallas kernels  49.3 us (31%)
  matrix products  13.6 us (9%)
  between operations  13.5 us (9%)
  starting transfers between devices  9.04 us (6%)
  local copies, waits for them, and re-layouts  4.56 us (3%)
  other arithmetic  4.3 us (3%)
    pallas_call x2, Pallas kernels, attend(): pl.pallas_call(functools.partial(attend_kernel, part, chunks, local_heads...  45.8 us
    all_gather x1, waiting for transfers between devices, shards(): lax.all_gather(pack_blocks(keys, values, picked, kv_heads), 'ctx', axis=0)  42.1 us
    ppermute x2, waiting for transfers between devices, shards(): arrived = lax.ppermute(away, 'kvh', [(0, 1), (1, 0)])  21.4 us
    dot_general x2, matrix products, shards(): mixed = jnp.dot(attended, out_weight, preferred_element_type=jnp.float32)  13.6 us
    ppermute x2, starting transfers between devices, shifted(): return lax.ppermute(value, axis, pairs)  6.89 us
    pallas_call x1, Pallas kernels, pack_blocks(): pl.pallas_call(pack_kernel, grid_spec=pltpu.PrefetchScalarGridSpec(num_sc...  3.53 us
  transfers between devices with their start and end apart: 5, of which 2 were waited for; matrix products, arithmetic and copies ran while one was open for 7% of the time, Pallas kernels for 14%

commit v1 on v0

--- a/solution.py
+++ b/solution.py
@@ -15,42 +15,188 @@
 WIN = 512
 WB = WIN // BLK
 NEAR = WIN + BLK
-PARTS = 2
+PARTS = (2, 1, 1)
+LANES = 4
+UP, SIDE, PAIRED, DIAGONAL = range(4)
 PAIR = 2
 EXP2_SCALE = math.log2(math.e) / math.sqrt(HD)
 
 masked_score = -1e30
 
 
-def shifted(value, axis, by):
-    devices = lax.axis_size(axis)
-    pairs = [(i, i + by) for i in range(devices) if 0 <= i + by < devices]
-    return lax.ppermute(value, axis, pairs)
-
-
-def pack_kernel(picked_ref, key_ref, value_ref, out_ref):
-    out_ref[0, :, :HD] = key_ref[...]
-    out_ref[0, :, HD:] = value_ref[...]
-
-
-def pack_blocks(keys, values, picked, kv_heads):
-    def source(kv, slot, picked_ref):
-        return picked_ref[kv * CAP + slot], kv
-
+def gather_kernel(
+    shard_count, picked_ref, keys_ref, values_ref,
+    pool_ref, earlier_keys_ref, earlier_values_ref,
+    packed, send, recv, window_send, window_recv, local,
+):
+    planes = shard_count // LANES
+    me = lax.axis_index("ctx")
+    plane, lane = lax.div(me, LANES), lax.rem(me, LANES)
+    other_lane = lax.rem(lane + 2, LANES)
+    across = plane * LANES + other_lane
+    twin = me + 1 - 2 * lax.rem(me, 2)
+    mesh_id = pl.DeviceIdType.MESH
+    below, above = plane > 0, plane < planes - 1
+    has_earlier, has_later = me > 0, me < shard_count - 1
+
+    barrier = pltpu.get_barrier_semaphore()
+
+    def greet(to):
+        pl.semaphore_signal(barrier, inc=1, device_id={"ctx": to}, device_id_type=mesh_id)
+
+    greet(across)
+    greet(twin)
+    beyond = me - 1 + 2 * lax.rem(me, 2)
+    has_beyond = (beyond >= 0) & (beyond < shard_count)
+    for there, to in ((below, me - LANES), (above, me + LANES), (has_beyond, beyond)):
+        pl.when(there)(functools.partial(greet, to))
+    kv_heads = packed.shape[0]
+    for kv in range(kv_heads):
+        lanes = slice(kv * HD, (kv + 1) * HD)
+        for slot in range(CAP):
+            chosen = jnp.full((BLK, HD), picked_ref[kv * CAP + slot], jnp.int32)
+            out = slice(slot * BLK, (slot + 1) * BLK)
+            for ref, start in ((keys_ref, 0), (values_ref, HD)):
+                tile = ref[:BLK, lanes].astype(jnp.float32)
+                for block in range(1, ref.shape[0] // BLK):
+                    own_tile = ref[block * BLK : (block + 1) * BLK, lanes].astype(jnp.float32)
+                    tile = jnp.where(chosen == block, own_tile, tile)
+                packed[kv, out, start : start + HD] = tile.astype(packed.dtype)
+    peers = jnp.int32(2)
+    for there in (below, above, has_beyond):
+        peers = peers + jnp.where(there, 1, 0).astype(jnp.int32)
+    pl.semaphore_wait(barrier, peers)
+
+    def move(kind, k, slot, to, arrival):
+        source = packed if k == 0 and kind != DIAGONAL else pool_ref.at[slot]
+        return pltpu.make_async_remote_copy(
+            src_ref=source, dst_ref=pool_ref.at[slot],
+            send_sem=send.at[kind, k], recv_sem=recv.at[kind, arrival],
+            device_id={"ctx": to}, device_id_type=mesh_id,
+        )
+
+    def up(k):
+        return move(UP, k, (plane - k) * LANES + lane, me + LANES, k + 1)
+
+    def side(k):
+        return move(SIDE, k, (plane - k) * LANES + lane, across, k)
+
+    def pair(k):
+        return move(PAIRED, k, (plane - k) * LANES + lane, twin, k)
+
+    def diagonal(k):
+        return move(DIAGONAL, k, (plane - k) * LANES + other_lane, twin, k)
+
+    def window(i):
+        source, target = ((keys_ref, earlier_keys_ref), (values_ref, earlier_values_ref))[i]
+        return pltpu.make_async_remote_copy(
+            src_ref=source, dst_ref=target,
+            send_sem=window_send.at[i], recv_sem=window_recv.at[i],
+            device_id={"ctx": me + 1}, device_id_type=mesh_id,
+        )
+
+    def arrived(kind, k, from_lane):
+        slot = (plane - k) * LANES + from_lane
+        pltpu.make_async_remote_copy(
+            src_ref=packed, dst_ref=pool_ref.at[slot],
+            send_sem=send.at[kind, k], recv_sem=recv.at[kind, k],
+            device_id={"ctx": twin}, device_id_type=mesh_id,
+        ).wait_recv()
+
+    twin_lane = lane + 1 - 2 * lax.rem(me, 2)
+    own = pltpu.make_async_copy(packed, pool_ref.at[me], local.at[0])
+    own.start()
+
+    fill = [
+        pltpu.make_async_copy(keys_ref, earlier_keys_ref, local.at[1]),
+        pltpu.make_async_copy(values_ref, earlier_values_ref, local.at[2]),
+    ]
+
+    @pl.when(jnp.logical_not(has_earlier))
+    def _():
+        for copy in fill:
+            copy.start()
+        for copy in fill:
+            copy.wait()
+
+    def stage(k):
+        if k > 0:
+            arrived(UP, k, lane)
+        pl.when(above)(lambda: up(k).start()) if k < planes - 1 else None
+        side(k).start()
+        pair(k).start()
+
+    def forward(k):
+        arrived(SIDE, k, other_lane)
+        diagonal(k).start()
+
+    for k in range(planes):
+        pl.when(plane >= k)(functools.partial(stage, k))
+        if k == 0:
+
+            @pl.when(has_later)
+            def _():
+                window(0).start()
+                window(1).start()
+
+        else:
+            pl.when(plane >= k - 1)(functools.partial(forward, k - 1))
+    pl.when(plane >= planes - 1)(functools.partial(forward, planes - 1))
+
+    def finish(k):
+        arrived(PAIRED, k, twin_lane)
+        arrived(DIAGONAL, k, lax.rem(twin_lane + 2, LANES))
+        side(k).wait_send()
+        pair(k).wait_send()
+        diagonal(k).wait_send()
+        if k < planes - 1:
+            pl.when(above)(lambda: up(k).wait_send())
+
+    for k in range(planes):
+        pl.when(plane >= k)(functools.partial(finish, k))
+    own.wait()
+
+    @pl.when(has_earlier)
+    def _():
+        window(0).wait_recv()
+        window(1).wait_recv()
+
+    @pl.when(has_later)
+    def _():
+        window(0).wait_send()
+        window(1).wait_send()
+
+
+def gather(picked, keys, values):
+    shard_count = lax.axis_size("ctx")
+    planes = shard_count // LANES
+    kv_heads = keys.shape[1] // HD
+    whole = pl.BlockSpec(memory_space=pltpu.VMEM)
+    anywhere = pl.BlockSpec(memory_space=pl.ANY)
+    block = (kv_heads, CAP * BLK, 2 * HD)
     return pl.pallas_call(
-        pack_kernel,
-        grid_spec=pltpu.PrefetchScalarGridSpec(
-            num_scalar_prefetch=1,
-            grid=(kv_heads, CAP),
-            in_specs=[pl.BlockSpec((BLK, HD), source), pl.BlockSpec((BLK, HD), source)],
-            out_specs=pl.BlockSpec((1, BLK, 2 * HD), lambda kv, slot, _: (kv, slot, 0)),
-        ),
-        out_shape=jax.ShapeDtypeStruct((kv_heads, CAP * BLK, 2 * HD), keys.dtype),
+        functools.partial(gather_kernel, shard_count),
+        out_shape=[
+            jax.ShapeDtypeStruct((shard_count,) + block, keys.dtype),
+            jax.ShapeDtypeStruct(keys.shape, keys.dtype),
+            jax.ShapeDtypeStruct(values.shape, values.dtype),
+        ],
+        in_specs=[pl.BlockSpec(memory_space=pltpu.SMEM), whole, whole],
+        out_specs=[anywhere, anywhere, anywhere],
+        scratch_shapes=[
+            pltpu.VMEM(block, keys.dtype),
+            pltpu.SemaphoreType.DMA((4, planes)),
+            pltpu.SemaphoreType.DMA((4, planes)),
+            pltpu.SemaphoreType.DMA((2,)),
+            pltpu.SemaphoreType.DMA((2,)),
+            pltpu.SemaphoreType.DMA((3,)),
+        ],
+        compiler_params=pltpu.CompilerParams(collective_id=0, has_side_effects=True),
     )(picked.reshape(-1), keys, values)
 
 
 def attend_kernel(
-    part, chunks, group_size,
+    first, chunks, group_size,
     columns_ref, rank_ref, query_ref, band_ref, pool_ref,
     earlier_keys_ref, keys_ref, earlier_values_ref, values_ref,
     out_ref,
@@ -60,7 +206,6 @@
     shard = lax.axis_index("ctx")
     kv_heads = window_k.shape[0]
     block_count = pool_ref.shape[0] * WB
-    first = part * chunks
 
     @pl.when(step == 0)
     def _():
@@ -89,10 +234,11 @@
         for n in range(NV):
             block = columns_ref[head * NV + n]
             blocks.append(block)
-            rank = rank_ref[kv * block_count + block]
+            source = jnp.minimum(block // WB, shard)
+            rank = jnp.minimum(rank_ref[kv * block_count + block], CAP - 1)
             rows = pl.ds(pl.multiple_of(rank * BLK, BLK), BLK)
-            far_k[pair, n * BLK : (n + 1) * BLK] = pool_ref[block // WB, kv, rows, :HD]
-            far_v[pair, n * BLK : (n + 1) * BLK, :HD] = pool_ref[block // WB, kv, rows, HD:]
+            far_k[pair, n * BLK : (n + 1) * BLK] = pool_ref[source, kv, rows, :HD]
+            far_v[pair, n * BLK : (n + 1) * BLK, :HD] = pool_ref[source, kv, rows, HD:]
         band = pltpu.roll(
             jnp.broadcast_to(band_ref[pair], (BLK, NEAR + BLK)), 0, 1, stride=1, stride_axis=0
         )[:, :NEAR]
@@ -168,20 +314,19 @@
             ).astype(jnp.bfloat16)
 
 
-def attend(part, queries, band, pool, columns, rank, earlier_keys, keys, earlier_values, values):
-    shard_rows, width = queries.shape
-    rows = shard_rows // PARTS
-    chunks = rows // BLK
+def attend(first, chunks, queries, band, pool, columns, rank, earlier_keys, keys, earlier_values, values):
+    width = queries.shape[1]
+    rows = chunks * BLK
     local_heads = width // HD
     kv_heads = keys.shape[1] // HD
     whole = pl.BlockSpec(memory_space=pltpu.VMEM)
     return pl.pallas_call(
-        functools.partial(attend_kernel, part, chunks, local_heads // kv_heads),
+        functools.partial(attend_kernel, first, chunks, local_heads // kv_heads),
         grid_spec=pltpu.PrefetchScalarGridSpec(
             num_scalar_prefetch=2,
             grid=(local_heads // PAIR,),
             in_specs=[
-                pl.BlockSpec((rows, PAIR * HD), lambda k, *_: (part, k)),
+                pl.BlockSpec((rows, PAIR * HD), lambda k, *_: (first // chunks, k)),
                 pl.BlockSpec((PAIR, 1, NEAR + BLK), lambda k, *_: (k, 0, 0)),
                 whole, whole, whole, whole, whole,
             ],
@@ -214,7 +359,6 @@
     owned = shard_rows // BLK
     shard_count = lax.axis_size("ctx")
     shard_index = lax.axis_index("ctx")
-    earlier_keys, earlier_values = shifted((keys, values), "ctx", 1)
 
     block_lane = jnp.arange(shard_count * owned, dtype=jnp.int32)
     listed = jnp.any(
@@ -229,7 +373,7 @@
     picked = jnp.sum(
         jnp.where(chosen, jnp.arange(owned, dtype=jnp.int32)[None, None, :], 0), axis=2
     )
-    pool = lax.all_gather(pack_blocks(keys, values, picked, kv_heads), "ctx", axis=0)
+    pool, earlier_keys, earlier_values = gather(picked, keys, values)
 
     distance = WIN - jnp.arange(NEAR + BLK, dtype=jnp.int32)
     band = jnp.where(
@@ -239,9 +383,10 @@
     half = out_weight.shape[1] // 2
     upper = lax.axis_index("kvh") == 1
     results = []
-    for part in range(PARTS):
+    first = 0
+    for chunks in PARTS:
         attended = attend(
-            part, queries, band, pool, columns, rank,
+            first, chunks, queries, band, pool, columns, rank,
             earlier_keys, keys, earlier_values, values,
         )
         mixed = jnp.dot(attended, out_weight, preferred_element_type=jnp.float32)
@@ -249,6 +394,7 @@
         away = jnp.where(upper, low, high).astype(jnp.bfloat16)
         home = jnp.where(upper, high, low)
         arrived = lax.ppermute(away, "kvh", [(0, 1), (1, 0)])
+        first += chunks
         results.append((home + arrived.astype(jnp.float32)).astype(jnp.bfloat16))
     return jnp.concatenate(results, axis=0)
 

time: 158 us -> 143 us (0.905)
  the two profiles are of different devices: /device:TPU:0 before, /device:TPU:24 now
where the time goes in v1:
time: 143 us
  Pallas kernels  89.9 us (63%)
  matrix products  20.1 us (14%)
  waiting for transfers between devices  20.1 us (14%)
  local copies, waits for them, and re-layouts  4.47 us (3%)
  other arithmetic  4.24 us (3%)
  starting transfers between devices  3.74 us (3%)
    pallas_call x3, Pallas kernels, attend(): pl.pallas_call(functools.partial(attend_kernel, first, chunks, local_head...  54.6 us
    pallas_call x1, Pallas kernels, gather(): pl.pallas_call(functools.partial(gather_kernel, shard_count), out_shape=[...  35.3 us
    dot_general x3, matrix products, shards(): mixed = jnp.dot(attended, out_weight, preferred_element_type=jnp.float32)  20.1 us
    ppermute x3, waiting for transfers between devices, shards(): arrived = lax.ppermute(away, 'kvh', [(0, 1), (1, 0)])  20.1 us
    ppermute x3, starting transfers between devices, shards(): arrived = lax.ppermute(away, 'kvh', [(0, 1), (1, 0)])  3.74 us
  transfers between devices with their start and end apart: 3, of which 1 were waited for; matrix products, arithmetic and copies ran while one was open for 10% of the time, Pallas kernels for 27%

profile of v1, /device:TPU:24, one launch (start us, length us, event | category | flops | bytes accessed | tf_op | source)
XLA Modules:
  0.0 142.6 jit_solution(16990831646368791455)
XLA Ops:
  0.0 1.3 reshape.52.columns_ref
  1.3 0.8 eq.47
  2.1 0.1 fusion
  2.2 0.1 reshape.55
  2.3 0.1 copy.11
  2.4 0.1 multiply_reduce_fusion
  2.5 0.2 dynamic-slice_reduce_fusion
  2.7 0.1 copy.12
  2.8 0.2 fusion.1
  2.9 0.6 reshape.54.picked_ref
  3.6 0.7 reshape.53.rank_ref
  4.2 1.6 %compare_reduce_fusion = pred[14,768]{1,0:T(8,128)(4,1)S(1)} fusion(s32[768]{0:T(1024)S(1)} %iota_subtract_fusion, s32[14,128]{1,0:T(8,128)} %param.10), kind=kLoop, calls=%fused_computation | loop fusion | flops 2741760 | bytes 20992 | tf_op jit(solution)/shard_map/reduce_or | solution.py:380
  5.9 0.6 select_n.57.band_ref
  6.5 35.3 %shard_map.64 = (bf16[16,2,256,256]{3,2,1,0:T(8,128)(2,1)}, bf16[512,256]{1,0:T(8,128)(2,1)}, bf16[512,256]{1,0:T(8,128)(2,1)}) custom-call(s32[4]{0:T(128)} %reshape.54.picked_ref, bf16[512,256]{1,0:T(8,128)(2,1)} %keys_ref.7, bf16[512,256]{1,0:T(8,128)(2,1)} %values_ref.7), custom_call_target="tpu_custom_call" | custom-call | tf_op jit(solution)/shard_map/pallas_call | solution.py:177
  41.8 16.0 %shard_map.66 = bf16[128,1792]{1,0:T(8,128)(2,1)} custom-call(s32[224]{0:T(256)} %reshape.52.columns_ref, s32[128]{0:T(128)} %reshape.53.rank_ref, bf16[512,1792]{1,0:T(8,128)(2,1)} %query_ref.5, f32[14,1,768]{2,1,0:T(1,128)} %select_n.57.band_ref, bf16[16,2,256,256]{3,2,1,0:T(8,128)(2,1)} %get-tuple-element.8.pool_ref, ...), custom_call_target="tpu_custom_call" | custom-call | flops 2466250752 | bytes 5111808 | tf_op jit(solution)/shard_map/pallas_call | solution.py:323
  57.9 6.7 %fusion.4 = f32[128,3584]{1,0:T(8,128)S(1)} fusion(bf16[128,1792]{1,0:T(8,128)(2,1)} %shard_map.66, bf16[1792,3584]{1,0:T(8,128)(2,1)} %param.11), kind=kOutput, calls=%fused_computation.21 | convolution fusion | flops 1644167168 | bytes 15138816 | tf_op jit(solution)/shard_map/dot_general | solution.py:392
  64.5 0.1 select_convert_fusion.2
  64.6 1.6 %collective-permute-start.1 = (bf16[128,1792]{1,0:T(8,128)(2,1)S(1)}, bf16[128,1792]{1,0:T(8,128)(2,1)S(1)}, u32[]{:S(2)}, u32[]{:S(2)}) collective-permute-start(bf16[128,1792]{1,0:T(8,128)(2,1)S(1)} %select_convert_fusion.2), channel_id=1, source_target_pairs={{0,1},{1,0},{2,3},{3,2},{4,5},{5,4},{6,7},{7,6},{8,9},{9,8},{10,11... | collective-permute-start | bytes 1376264 | tf_op jit(solution)/shard_map/ppermute | solution.py:396
  66.2 15.9 %shard_map.67 = bf16[128,1792]{1,0:T(8,128)(2,1)} custom-call(s32[224]{0:T(256)} %reshape.52.columns_ref, s32[128]{0:T(128)} %reshape.53.rank_ref, bf16[512,1792]{1,0:T(8,128)(2,1)} %query_ref.5, f32[14,1,768]{2,1,0:T(1,128)} %select_n.57.band_ref, bf16[16,2,256,256]{3,2,1,0:T(8,128)(2,1)} %get-tuple-element.8.pool_ref, ...), custom_call_target="tpu_custom_call" | custom-call | flops 2466250752 | bytes 5111808 | tf_op jit(solution)/shard_map/pallas_call | solution.py:323
  82.1 6.6 %fusion.5 = f32[128,3584]{1,0:T(8,128)S(1)} fusion(bf16[128,1792]{1,0:T(8,128)(2,1)} %shard_map.67, bf16[1792,3584]{1,0:T(8,128)(2,1)} %param.11), kind=kOutput, calls=%fused_computation.22 | convolution fusion | flops 1644167168 | bytes 15138816 | tf_op jit(solution)/shard_map/dot_general | solution.py:392
  88.7 0.1 select_convert_fusion.1
  88.8 0.6 collective-permute-start.2
  89.4 22.7 %shard_map.65 = bf16[256,1792]{1,0:T(8,128)(2,1)} custom-call(s32[224]{0:T(256)} %reshape.52.columns_ref, s32[128]{0:T(128)} %reshape.53.rank_ref, bf16[512,1792]{1,0:T(8,128)(2,1)} %query_ref.5, f32[14,1,768]{2,1,0:T(1,128)} %select_n.57.band_ref, bf16[16,2,256,256]{3,2,1,0:T(8,128)(2,1)} %get-tuple-element.8.pool_ref, ...), custom_call_target="tpu_custom_call" | custom-call | flops 4932501504 | bytes 6029312 | tf_op jit(solution)/shard_map/pallas_call | solution.py:323
  112.1 6.8 %fusion.3 = f32[256,3584]{1,0:T(8,128)S(1)} fusion(bf16[256,1792]{1,0:T(8,128)(2,1)} %shard_map.65, bf16[1792,3584]{1,0:T(8,128)(2,1)} %param.11), kind=kOutput, calls=%fused_computation.20 | convolution fusion | flops 3288334336 | bytes 17432576 | tf_op jit(solution)/shard_map/dot_general | solution.py:392
  118.9 0.2 select_convert_fusion
  119.0 1.6 %collective-permute-start = (bf16[256,1792]{1,0:T(8,128)(2,1)S(1)}, bf16[256,1792]{1,0:T(8,128)(2,1)S(1)}, u32[]{:S(2)}, u32[]{:S(2)}) collective-permute-start(bf16[256,1792]{1,0:T(8,128)(2,1)S(1)} %select_convert_fusion), channel_id=1, source_target_pairs={{0,1},{1,0},{2,3},{3,2},{4,5},{5,4},{6,7},{7,6},{8,9},{9,8},{10,11... | collective-permute-start | bytes 2752520 | tf_op jit(solution)/shard_map/ppermute | solution.py:396
  120.6 0.0 collective-permute-done.1
  120.6 0.1 add_convert_fusion.2
  120.7 0.0 collective-permute-done.2
  120.7 0.1 add_convert_fusion.1
  120.9 20.1 %collective-permute-done = bf16[256,1792]{1,0:T(8,128)(2,1)S(1)} collective-permute-done((bf16[256,1792]{1,0:T(8,128)(2,1)S(1)}, bf16[256,1792]{1,0:T(8,128)(2,1)S(1)}, u32[]{:S(2)}, u32[]{:S(2)}) %collective-permute-start) | collective-permute-done | bytes 917536 | tf_op jit(solution)/shard_map/ppermute | solution.py:396
  140.9 0.3 add_convert_fusion
  141.3 1.4 pad_maximum_fusion
  (6 shorter events, 0.0 us)
Async XLA Ops:
  64.6 56.0 %collective-permute-start.1 = (bf16[128,1792]{1,0:T(8,128)(2,1)S(1)}, bf16[128,1792]{1,0:T(8,128)(2,1)S(1)}, u32[]{:S(2)}, u32[]{:S(2)}) collective-permute-start(bf16[128,1792]{1,0:T(8,128)(2,1)S(1)} %select_convert_fusion.2), channel_id=1, source_target_pairs={{0,1},{1,0},{2,3},{3,2},{4,5},{5,4},{6,7},{7,6},{8,9},{9,8},{10,11... | collective-permute-start | bytes 1376264 | tf_op jit(solution)/shard_map/ppermute | solution.py:396
  88.8 31.9 %collective-permute-start.2 = (bf16[128,1792]{1,0:T(8,128)(2,1)S(1)}, bf16[128,1792]{1,0:T(8,128)(2,1)S(1)}, u32[]{:S(2)}, u32[]{:S(2)}) collective-permute-start(bf16[128,1792]{1,0:T(8,128)(2,1)S(1)} %select_convert_fusion.1), channel_id=1, source_target_pairs={{0,1},{1,0},{2,3},{3,2},{4,5},{5,4},{6,7},{7,6},{8,9},{9,8},{10,11... | collective-permute-start | bytes 1376264 | tf_op jit(solution)/shard_map/ppermute | solution.py:396
  119.0 21.9 %collective-permute-start = (bf16[256,1792]{1,0:T(8,128)(2,1)S(1)}, bf16[256,1792]{1,0:T(8,128)(2,1)S(1)}, u32[]{:S(2)}, u32[]{:S(2)}) collective-permute-start(bf16[256,1792]{1,0:T(8,128)(2,1)S(1)} %select_convert_fusion), channel_id=1, source_target_pairs={{0,1},{1,0},{2,3},{3,2},{4,5},{5,4},{6,7},{7,6},{8,9},{9,8},{10,11... | collective-permute-start | bytes 2752520 | tf_op jit(solution)/shard_map/ppermute | solution.py:396

commit v2 on v1

--- a/solution.py
+++ b/solution.py
@@ -15,7 +15,7 @@
 WIN = 512
 WB = WIN // BLK
 NEAR = WIN + BLK
-PARTS = (2, 1, 1)
+PARTS = (2, 2)
 LANES = 4
 UP, SIDE, PAIRED, DIAGONAL = range(4)
 PAIR = 2
@@ -198,17 +198,21 @@
 def attend_kernel(
     first, chunks, group_size,
     columns_ref, rank_ref, query_ref, band_ref, pool_ref,
-    earlier_keys_ref, keys_ref, earlier_values_ref, values_ref,
-    out_ref,
-    window_k, window_v, far_k, far_v, far_s, near_s, far_p, near_p,
+    earlier_keys_ref, keys_ref, earlier_values_ref, values_ref, weight_ref,
+    out_ref, away_ref,
+    attended, away_weight, weight_sem, window_k, window_v, far_k, far_v, far_s, near_s, far_p, near_p,
 ):
     step = pl.program_id(0)
     shard = lax.axis_index("ctx")
     kv_heads = window_k.shape[0]
     block_count = pool_ref.shape[0] * WB
+    half = away_weight.shape[1]
+    away_lanes = pl.ds(pl.multiple_of((1 - lax.axis_index("kvh")) * half, HD), half)
+    weight_copy = pltpu.make_async_copy(weight_ref.at[:, away_lanes], away_weight, weight_sem)
 
     @pl.when(step == 0)
     def _():
+        weight_copy.start()
         ones = jnp.ones((2 * WIN, HD), jnp.bfloat16)
         for kv in range(kv_heads):
             lanes = slice(kv * HD, (kv + 1) * HD)
@@ -309,14 +313,58 @@
                 window_v[kv, (first + a) * BLK : (first + a) * BLK + NEAR],
                 preferred_element_type=jnp.float32,
             )
-            out_ref[rows, pair * HD : (pair + 1) * HD] = (
-                sums[:, :HD] / sums[:, HD:]
-            ).astype(jnp.bfloat16)
-
-
-def attend(first, chunks, queries, band, pool, columns, rank, earlier_keys, keys, earlier_values, values):
+            result = (sums[:, :HD] / sums[:, HD:]).astype(jnp.bfloat16)
+            out_ref[rows, pair * HD : (pair + 1) * HD] = result
+            attended[rows, pl.ds(pl.multiple_of(head * HD, HD), HD)] = result
+
+    @pl.when(step == pl.num_programs(0) - 1)
+    def _():
+        weight_copy.wait()
+        for start in range(0, half, 2 * HD):
+            lanes = slice(start, start + 2 * HD)
+            away_ref[:, lanes] = jnp.dot(
+                attended[...], away_weight[:, lanes], preferred_element_type=jnp.float32
+            ).astype(away_ref.dtype)
+
+
+def home_kernel(index_ref, *refs):
+    count = (len(refs) - 1) // 2
+    weight = refs[count][...]
+    for part in range(count):
+        refs[count + 1 + part][...] = jnp.dot(
+            refs[part][...], weight, preferred_element_type=jnp.float32
+        )
+
+
+def project_home(parts, out_weight):
+    depth, width = out_weight.shape
+    tile = 2 * HD
+    tiles = width // 2 // tile
+    index = lax.axis_index("kvh").astype(jnp.int32).reshape(1)
+    rows = [part.shape[0] for part in parts]
+    return pl.pallas_call(
+        home_kernel,
+        grid_spec=pltpu.PrefetchScalarGridSpec(
+            num_scalar_prefetch=1,
+            grid=(tiles,),
+            in_specs=[pl.BlockSpec((r, depth), lambda j, _: (0, 0)) for r in rows]
+            + [pl.BlockSpec((depth, tile), lambda j, index_ref: (0, index_ref[0] * tiles + j))],
+            out_specs=[pl.BlockSpec((r, tile), lambda j, _: (0, j)) for r in rows],
+        ),
+        out_shape=[jax.ShapeDtypeStruct((r, width // 2), jnp.float32) for r in rows],
+        compiler_params=pltpu.CompilerParams(vmem_limit_bytes=32 * 1024 * 1024),
+        cost_estimate=pl.CostEstimate(
+            flops=sum(rows) * depth * width,
+            bytes_accessed=depth * width + sum(rows) * (2 * depth + 2 * width),
+            transcendentals=0,
+        ),
+    )(index, *parts, out_weight)
+
+
+def attend(first, chunks, queries, band, pool, columns, rank, earlier_keys, keys, earlier_values, values, out_weight):
     width = queries.shape[1]
     rows = chunks * BLK
+    half = out_weight.shape[1] // 2
     local_heads = width // HD
     kv_heads = keys.shape[1] // HD
     whole = pl.BlockSpec(memory_space=pltpu.VMEM)
@@ -329,9 +377,16 @@
                 pl.BlockSpec((rows, PAIR * HD), lambda k, *_: (first // chunks, k)),
                 pl.BlockSpec((PAIR, 1, NEAR + BLK), lambda k, *_: (k, 0, 0)),
                 whole, whole, whole, whole, whole,
+                pl.BlockSpec(memory_space=pl.ANY),
             ],
-            out_specs=pl.BlockSpec((rows, PAIR * HD), lambda k, *_: (0, k)),
+            out_specs=[
+                pl.BlockSpec((rows, PAIR * HD), lambda k, *_: (0, k)),
+                pl.BlockSpec((rows, half), lambda k, *_: (0, 0)),
+            ],
             scratch_shapes=[
+                pltpu.VMEM((rows, width), jnp.bfloat16),
+                pltpu.VMEM((width, half), jnp.bfloat16),
+                pltpu.SemaphoreType.DMA,
                 pltpu.VMEM((kv_heads, 2 * WIN, HD), jnp.bfloat16),
                 pltpu.VMEM((kv_heads, 2 * WIN, 2 * HD), jnp.bfloat16),
                 pltpu.VMEM((PAIR, NV * BLK, HD), jnp.bfloat16),
@@ -342,7 +397,10 @@
                 pltpu.VMEM((PAIR, rows, NEAR), jnp.bfloat16),
             ],
         ),
-        out_shape=jax.ShapeDtypeStruct((rows, width), jnp.bfloat16),
+        out_shape=[
+            jax.ShapeDtypeStruct((rows, width), jnp.bfloat16),
+            jax.ShapeDtypeStruct((rows, half), jnp.bfloat16),
+        ],
         compiler_params=pltpu.CompilerParams(vmem_limit_bytes=56 * 1024 * 1024),
         cost_estimate=pl.CostEstimate(
             flops=4 * rows * (NV * BLK + NEAR) * width,
@@ -350,7 +408,7 @@
             transcendentals=rows * (NV * BLK + NEAR) * local_heads,
         ),
     )(columns.reshape(-1), rank.reshape(-1), queries, band, pool,
-      earlier_keys, keys, earlier_values, values)
+      earlier_keys, keys, earlier_values, values, out_weight)
 
 
 def shards(queries, keys, values, columns, offsets, out_weight):
@@ -380,23 +438,21 @@
         jnp.any(offsets[:, :, None] == distance[None, None, :], axis=1), 0.0, masked_score
     ).astype(jnp.float32)[:, None, :]
 
-    half = out_weight.shape[1] // 2
-    upper = lax.axis_index("kvh") == 1
-    results = []
     first = 0
+    parts, arrivals = [], []
     for chunks in PARTS:
-        attended = attend(
+        attended, away = attend(
             first, chunks, queries, band, pool, columns, rank,
-            earlier_keys, keys, earlier_values, values,
+            earlier_keys, keys, earlier_values, values, out_weight,
         )
-        mixed = jnp.dot(attended, out_weight, preferred_element_type=jnp.float32)
-        low, high = mixed[:, :half], mixed[:, half:]
-        away = jnp.where(upper, low, high).astype(jnp.bfloat16)
-        home = jnp.where(upper, high, low)
-        arrived = lax.ppermute(away, "kvh", [(0, 1), (1, 0)])
+        parts.append(attended)
+        arrivals.append(lax.ppermute(away, "kvh", [(0, 1), (1, 0)]))
         first += chunks
-        results.append((home + arrived.astype(jnp.float32)).astype(jnp.bfloat16))
-    return jnp.concatenate(results, axis=0)
+    home = project_home(parts, out_weight)
+    return jnp.concatenate(
+        [(own + far.astype(jnp.float32)).astype(jnp.bfloat16) for own, far in zip(home, arrivals)],
+        axis=0,
+    )
 
 
 def solution(mesh):

time: 143 us -> 118 us (0.83)
  matrix products: 20.1 us -> 0 us
  waiting for transfers between devices: 20.1 us -> 10.5 us
  local copies, waits for them, and re-layouts: 4.47 us -> 10.2 us
  starting transfers between devices: 3.74 us -> 2.16 us
    dot_general x3 -> x0, matrix products: 20.1 us -> none  [shards(): mixed = jnp.dot(attended, out_weight, preferred_element_type=jnp.float32)]
    ppermute x3 -> x2, waiting for transfers between devices: 20.1 us -> 10.5 us  [shards(): arrivals.append(lax.ppermute(away, 'kvh', [(0, 1), (1, 0)]))]
    unnamed x1 -> x7, local copies, waits for them, and re-layouts: 0.01 us -> 5.84 us
    pallas_call x0 -> x1, Pallas kernels: none -> 5.22 us  [project_home(): pl.pallas_call(home_kernel, grid_spec=pltpu.PrefetchScalarGridSpec(num_sc...]
    pallas_call x3 -> x2, Pallas kernels: 54.6 us -> 50.2 us  [attend(): pl.pallas_call(functools.partial(attend_kernel, first, chunks, local_head...]
    ppermute x3 -> x2, starting transfers between devices: 3.74 us -> 2.16 us  [shards(): arrivals.append(lax.ppermute(away, 'kvh', [(0, 1), (1, 0)]))]
  transfers between devices with their start and end apart: 3 -> 2, of which waited for: 1 -> 1; matrix products, arithmetic and copies ran while one was open for 10% -> 0% of each run, Pallas kernels for 27% -> 26%
where the time goes in v2:
time: 118 us
  Pallas kernels  90.8 us (77%)
  waiting for transfers between devices  10.5 us (9%)
  local copies, waits for them, and re-layouts  10.2 us (9%)
  other arithmetic  3.76 us (3%)
  starting transfers between devices  2.16 us (2%)
    pallas_call x2, Pallas kernels, attend(): pl.pallas_call(functools.partial(attend_kernel, first, chunks, local_head...  50.2 us
    pallas_call x1, Pallas kernels, gather(): pl.pallas_call(functools.partial(gather_kernel, shard_count), out_shape=[...  35.3 us
    ppermute x2, waiting for transfers between devices, shards(): arrivals.append(lax.ppermute(away, 'kvh', [(0, 1), (1, 0)]))  10.5 us
    unnamed x7, local copies, waits for them, and re-layouts  5.84 us
    pallas_call x1, Pallas kernels, project_home(): pl.pallas_call(home_kernel, grid_spec=pltpu.PrefetchScalarGridSpec(num_sc...  5.22 us
  transfers between devices with their start and end apart: 2, of which 1 were waited for; matrix products, arithmetic and copies ran while one was open for 0% of the time, Pallas kernels for 26%

profile of v2, /device:TPU:24, one launch (start us, length us, event | category | flops | bytes accessed | tf_op | source)
XLA Modules:
  0.0 117.6 jit_solution(9453331174628805623)
XLA Ops:
  0.0 1.3 %reshape.54.columns_ref = s32[224]{0:T(256)} reshape(s32[14,16]{1,0:T(8,128)} %param.9) | data formatting | bytes 1792 | tf_op jit(solution)/shard_map/reshape | solution.py:410
  1.3 0.8 eq.43
  2.1 0.1 fusion
  2.2 0.1 reshape.57
  2.3 0.1 copy.11
  2.4 0.1 multiply_reduce_fusion
  2.5 0.2 dynamic-slice_reduce_fusion
  2.7 0.1 copy.12
  2.8 0.2 fusion.1
  3.0 0.6 reshape.56.picked_ref
  3.6 0.6 reshape.55.rank_ref
  4.2 1.6 %compare_reduce_fusion = pred[14,768]{1,0:T(8,128)(4,1)S(1)} fusion(s32[768]{0:T(1024)S(1)} %iota_subtract_fusion, s32[14,128]{1,0:T(8,128)} %param.10), kind=kLoop, calls=%fused_computation | loop fusion | flops 2741760 | bytes 20992 | tf_op jit(solution)/shard_map/reduce_or | solution.py:438
  5.8 0.6 select_n.24.band_ref
  6.5 35.3 %shard_map.64 = (bf16[16,2,256,256]{3,2,1,0:T(8,128)(2,1)}, bf16[512,256]{1,0:T(8,128)(2,1)}, bf16[512,256]{1,0:T(8,128)(2,1)}) custom-call(s32[4]{0:T(128)} %reshape.56.picked_ref, bf16[512,256]{1,0:T(8,128)(2,1)} %keys_ref.5, bf16[512,256]{1,0:T(8,128)(2,1)} %values_ref.5), custom_call_target="tpu_custom_call" | custom-call | tf_op jit(solution)/shard_map/pallas_call | solution.py:177
  41.8 25.1 %shard_map.65 = (bf16[256,1792]{1,0:T(8,128)(2,1)}, bf16[256,1792]{1,0:T(8,128)(2,1)}) custom-call(s32[224]{0:T(256)} %reshape.54.columns_ref, s32[128]{0:T(128)} %reshape.55.rank_ref, bf16[512,1792]{1,0:T(8,128)(2,1)} %query_ref.3, f32[14,1,768]{2,1,0:T(1,128)} %select_n.24.band_ref, bf16[16,2,256,256]{3,2,1,0:T(8,128)(2,1)} %get-tuple-element.14.pool_ref, ...), custom_call_target="tpu_custom_call" | custom-call | flops 4932501504 | bytes 6029312 | tf_op jit(solution)/shard_map/pallas_call | solution.py:371
  66.9 0.0 copy-start.1
  66.9 1.6 %collective-permute-start = (bf16[256,1792]{1,0:T(8,128)(2,1)}, bf16[256,1792]{1,0:T(8,128)(2,1)S(1)}, u32[]{:S(2)}, u32[]{:S(2)}) collective-permute-start(bf16[256,1792]{1,0:T(8,128)(2,1)} %get-tuple-element.20), channel_id=1, source_target_pairs={{0,1},{1,0},{2,3},{3,2},{4,5},{5,4},{6,7},{7,6},{8,9},{9,8},{10,11... | collective-permute-start | bytes 2752520 | tf_op jit(solution)/shard_map/ppermute | solution.py:449
  68.5 25.1 %shard_map.66 = (bf16[256,1792]{1,0:T(8,128)(2,1)}, bf16[256,1792]{1,0:T(8,128)(2,1)}) custom-call(s32[224]{0:T(256)} %reshape.54.columns_ref, s32[128]{0:T(128)} %reshape.55.rank_ref, bf16[512,1792]{1,0:T(8,128)(2,1)} %query_ref.3, f32[14,1,768]{2,1,0:T(1,128)} %select_n.24.band_ref, bf16[16,2,256,256]{3,2,1,0:T(8,128)(2,1)} %get-tuple-element.14.pool_ref, ...), custom_call_target="tpu_custom_call" | custom-call | flops 4932501504 | bytes 6029312 | tf_op jit(solution)/shard_map/pallas_call | solution.py:371
  93.6 0.6 collective-permute-start.1
  94.2 0.0 copy-done.1
  94.2 0.0 copy-start
  94.2 4.6 %copy-done = bf16[1792,3584]{1,0:T(8,128)(2,1)S(1)} copy-done((bf16[1792,3584]{1,0:T(8,128)(2,1)S(1)}, bf16[1792,3584]{1,0:T(8,128)(2,1)}, u32[]{:S(2)}) %copy-start) | copy-done | bytes 12845080
  98.9 0.0 copy-start.2
  98.9 1.2 %copy-done.2 = bf16[256,1792]{1,0:T(8,128)(2,1)S(1)} copy-done((bf16[256,1792]{1,0:T(8,128)(2,1)S(1)}, bf16[256,1792]{1,0:T(8,128)(2,1)}, u32[]{:S(2)}) %copy-start.2) | copy-done | bytes 917528
  100.0 5.2 %shard_map.67 = (f32[256,1792]{1,0:T(8,128)S(1)}, f32[256,1792]{1,0:T(8,128)S(1)}) custom-call(s32[1]{0:T(128)} %bitcast.index_ref, bf16[256,1792]{1,0:T(8,128)(2,1)S(1)} %copy-done.1, bf16[256,1792]{1,0:T(8,128)(2,1)S(1)} %copy-done.2, bf16[1792,3584]{1,0:T(8,128)(2,1)S(1)} %copy-done), custom_call_target="tpu_custom_call" | custom-call | flops 3288334336 | bytes 11927552 | tf_op jit(solution)/shard_map/pallas_call | solution.py:345
  105.3 0.0 collective-permute-done
  105.3 0.2 add_convert_fusion.1
  105.5 10.5 %collective-permute-done.1 = bf16[256,1792]{1,0:T(8,128)(2,1)S(1)} collective-permute-done((bf16[256,1792]{1,0:T(8,128)(2,1)}, bf16[256,1792]{1,0:T(8,128)(2,1)S(1)}, u32[]{:S(2)}, u32[]{:S(2)}) %collective-permute-start.1) | collective-permute-done | bytes 917536 | tf_op jit(solution)/shard_map/ppermute | solution.py:449
  116.0 0.2 add_convert_fusion
  116.2 1.3 %pad_maximum_fusion = bf16[512,1792]{1,0:T(8,128)(2,1)} fusion(bf16[256,1792]{1,0:T(8,128)(2,1)S(1)} %add_convert_fusion, bf16[256,1792]{1,0:T(8,128)(2,1)S(1)} %add_convert_fusion.1), kind=kLoop, calls=%fused_computation.1 | loop fusion | flops 3670016 | bytes 3670016 | tf_op jit(solution)/shard_map/concatenate | solution.py:452
  (6 shorter events, 0.0 us)
Async XLA Ops:
  66.9 27.3 %copy-start.1 = (bf16[256,1792]{1,0:T(8,128)(2,1)S(1)}, bf16[256,1792]{1,0:T(8,128)(2,1)}, u32[]{:S(2)}) copy-start(bf16[256,1792]{1,0:T(8,128)(2,1)} %get-tuple-element.17.refs_0_) | copy-start | bytes 2752516
  66.9 38.3 %collective-permute-start = (bf16[256,1792]{1,0:T(8,128)(2,1)}, bf16[256,1792]{1,0:T(8,128)(2,1)S(1)}, u32[]{:S(2)}, u32[]{:S(2)}) collective-permute-start(bf16[256,1792]{1,0:T(8,128)(2,1)} %get-tuple-element.20), channel_id=1, source_target_pairs={{0,1},{1,0},{2,3},{3,2},{4,5},{5,4},{6,7},{7,6},{8,9},{9,8},{10,11... | collective-permute-start | bytes 2752520 | tf_op jit(solution)/shard_map/ppermute | solution.py:449
  93.6 22.4 %collective-permute-start.1 = (bf16[256,1792]{1,0:T(8,128)(2,1)}, bf16[256,1792]{1,0:T(8,128)(2,1)S(1)}, u32[]{:S(2)}, u32[]{:S(2)}) collective-permute-start(bf16[256,1792]{1,0:T(8,128)(2,1)} %get-tuple-element.22), channel_id=1, source_target_pairs={{0,1},{1,0},{2,3},{3,2},{4,5},{5,4},{6,7},{7,6},{8,9},{9,8},{10,11... | collective-permute-start | bytes 2752520 | tf_op jit(solution)/shard_map/ppermute | solution.py:449
  94.2 4.7 %copy-start = (bf16[1792,3584]{1,0:T(8,128)(2,1)S(1)}, bf16[1792,3584]{1,0:T(8,128)(2,1)}, u32[]{:S(2)}) copy-start(bf16[1792,3584]{1,0:T(8,128)(2,1)} %refs_2_.1) | copy-start | bytes 38535172
  98.9 1.2 %copy-start.2 = (bf16[256,1792]{1,0:T(8,128)(2,1)S(1)}, bf16[256,1792]{1,0:T(8,128)(2,1)}, u32[]{:S(2)}) copy-start(bf16[256,1792]{1,0:T(8,128)(2,1)} %get-tuple-element.18.refs_1_) | copy-start | bytes 2752516

commit v3 on v2

--- a/solution.py
+++ b/solution.py
@@ -54,7 +54,7 @@
     for kv in range(kv_heads):
         lanes = slice(kv * HD, (kv + 1) * HD)
         for slot in range(CAP):
-            chosen = jnp.full((BLK, HD), picked_ref[kv * CAP + slot], jnp.int32)
+            chosen = jnp.full((BLK, HD), picked_ref[kv, slot], jnp.int32)
             out = slice(slot * BLK, (slot + 1) * BLK)
             for ref, start in ((keys_ref, 0), (values_ref, HD)):
                 tile = ref[:BLK, lanes].astype(jnp.float32)
@@ -192,7 +192,7 @@
             pltpu.SemaphoreType.DMA((3,)),
         ],
         compiler_params=pltpu.CompilerParams(collective_id=0, has_side_effects=True),
-    )(picked.reshape(-1), keys, values)
+    )(picked, keys, values)
 
 
 def attend_kernel(
@@ -205,7 +205,6 @@
     step = pl.program_id(0)
     shard = lax.axis_index("ctx")
     kv_heads = window_k.shape[0]
-    block_count = pool_ref.shape[0] * WB
     half = away_weight.shape[1]
     away_lanes = pl.ds(pl.multiple_of((1 - lax.axis_index("kvh")) * half, HD), half)
     weight_copy = pltpu.make_async_copy(weight_ref.at[:, away_lanes], away_weight, weight_sem)
@@ -236,10 +235,10 @@
         query = query_ref[:, pair * HD : (pair + 1) * HD]
         blocks = []
         for n in range(NV):
-            block = columns_ref[head * NV + n]
+            block = columns_ref[head, n]
             blocks.append(block)
             source = jnp.minimum(block // WB, shard)
-            rank = jnp.minimum(rank_ref[kv * block_count + block], CAP - 1)
+            rank = jnp.minimum(rank_ref[kv, block], CAP - 1)
             rows = pl.ds(pl.multiple_of(rank * BLK, BLK), BLK)
             far_k[pair, n * BLK : (n + 1) * BLK] = pool_ref[source, kv, rows, :HD]
             far_v[pair, n * BLK : (n + 1) * BLK, :HD] = pool_ref[source, kv, rows, HD:]
@@ -407,7 +406,7 @@
             bytes_accessed=2 * pool.size + 4 * rows * width,
             transcendentals=rows * (NV * BLK + NEAR) * local_heads,
         ),
-    )(columns.reshape(-1), rank.reshape(-1), queries, band, pool,
+    )(columns, rank.reshape(kv_heads, -1), queries, band, pool,
       earlier_keys, keys, earlier_values, values, out_weight)
 
 

time: 118 us -> 117 us (level)
  local copies, waits for them, and re-layouts: 10.2 us -> 8.38 us
    reshape x3 -> x1, local copies, waits for them, and re-layouts: 2.51 us -> 0.64 us  [attend(): rank.reshape(kv_heads, -1)]
where the time goes in v3:
time: 117 us
  Pallas kernels  91 us (78%)
  waiting for transfers between devices  10.5 us (9%)
  local copies, waits for them, and re-layouts  8.38 us (7%)
  other arithmetic  4.32 us (4%)
  starting transfers between devices  2.16 us (2%)
    pallas_call x2, Pallas kernels, attend(): pl.pallas_call(functools.partial(attend_kernel, first, chunks, local_head...  50.5 us
    pallas_call x1, Pallas kernels, gather(): pl.pallas_call(functools.partial(gather_kernel, shard_count), out_shape=[...  35.3 us
    ppermute x2, waiting for transfers between devices, shards(): arrivals.append(lax.ppermute(away, 'kvh', [(0, 1), (1, 0)]))  10.5 us
    unnamed x7, local copies, waits for them, and re-layouts  5.84 us
    pallas_call x1, Pallas kernels, project_home(): pl.pallas_call(home_kernel, grid_spec=pltpu.PrefetchScalarGridSpec(num_sc...  5.22 us
  transfers between devices with their start and end apart: 2, of which 1 were waited for; matrix products, arithmetic and copies ran while one was open for 0% of the time, Pallas kernels for 26%

profile of v3, /device:TPU:24, one launch (start us, length us, event | category | flops | bytes accessed | tf_op | source)
XLA Modules:
  0.0 116.5 jit_solution(18011421300815434551)
XLA Ops:
  0.0 0.8 eq.43
  0.8 0.1 fusion
  0.9 0.1 reshape.48
  1.0 0.1 copy.11
  1.1 0.1 multiply_reduce_fusion
  1.2 0.2 dynamic-slice_reduce_fusion
  1.4 0.1 copy.12
  1.5 0.6 reshape.47.rank_ref
  2.1 1.6 %compare_reduce_fusion = pred[14,768]{1,0:T(8,128)(4,1)S(1)} fusion(s32[768]{0:T(1024)S(1)} %iota_subtract_fusion, s32[14,128]{1,0:T(8,128)} %param.10), kind=kLoop, calls=%fused_computation | loop fusion | flops 2741760 | bytes 20992 | tf_op jit(solution)/shard_map/reduce_or | solution.py:437
  3.8 0.6 select_n.24.band_ref
  4.4 0.7 fusion.1.picked_ref
  5.2 35.3 %shard_map.64 = (bf16[16,2,256,256]{3,2,1,0:T(8,128)(2,1)}, bf16[512,256]{1,0:T(8,128)(2,1)}, bf16[512,256]{1,0:T(8,128)(2,1)}) custom-call(s32[2,2]{1,0:T(2,128)} %fusion.1.picked_ref, bf16[512,256]{1,0:T(8,128)(2,1)} %keys_ref.5, bf16[512,256]{1,0:T(8,128)(2,1)} %values_ref.5), custom_call_target="tpu_custom_call" | custom-call | tf_op jit(solution)/shard_map/pallas_call | solution.py:177
  40.5 25.2 %shard_map.65 = (bf16[256,1792]{1,0:T(8,128)(2,1)}, bf16[256,1792]{1,0:T(8,128)(2,1)}) custom-call(s32[14,16]{1,0:T(8,128)} %columns_ref.3, s32[2,64]{1,0:T(2,128)} %reshape.47.rank_ref, bf16[512,1792]{1,0:T(8,128)(2,1)} %query_ref.3, f32[14,1,768]{2,1,0:T(1,128)} %select_n.24.band_ref, bf16[16,2,256,256]{3,2,1,0:T(8,128)(2,1)} %get-tuple-element.14.pool_ref, ...), custom_call_target="tpu_custom_call" | custom-call | flops 4932501504 | bytes 6029312 | tf_op jit(solution)/shard_map/pallas_call | solution.py:370
  65.7 0.0 copy-start.1
  65.7 1.6 %collective-permute-start = (bf16[256,1792]{1,0:T(8,128)(2,1)}, bf16[256,1792]{1,0:T(8,128)(2,1)S(1)}, u32[]{:S(2)}, u32[]{:S(2)}) collective-permute-start(bf16[256,1792]{1,0:T(8,128)(2,1)} %get-tuple-element.20), channel_id=1, source_target_pairs={{0,1},{1,0},{2,3},{3,2},{4,5},{5,4},{6,7},{7,6},{8,9},{9,8},{10,11... | collective-permute-start | bytes 2752520 | tf_op jit(solution)/shard_map/ppermute | solution.py:448
  67.3 25.3 %shard_map.66 = (bf16[256,1792]{1,0:T(8,128)(2,1)}, bf16[256,1792]{1,0:T(8,128)(2,1)}) custom-call(s32[14,16]{1,0:T(8,128)} %columns_ref.3, s32[2,64]{1,0:T(2,128)} %reshape.47.rank_ref, bf16[512,1792]{1,0:T(8,128)(2,1)} %query_ref.3, f32[14,1,768]{2,1,0:T(1,128)} %select_n.24.band_ref, bf16[16,2,256,256]{3,2,1,0:T(8,128)(2,1)} %get-tuple-element.14.pool_ref, ...), custom_call_target="tpu_custom_call" | custom-call | flops 4932501504 | bytes 6029312 | tf_op jit(solution)/shard_map/pallas_call | solution.py:370
  92.6 0.6 collective-permute-start.1
  93.2 0.0 copy-done.1
  93.2 0.0 copy-start
  93.2 4.6 %copy-done = bf16[1792,3584]{1,0:T(8,128)(2,1)S(1)} copy-done((bf16[1792,3584]{1,0:T(8,128)(2,1)S(1)}, bf16[1792,3584]{1,0:T(8,128)(2,1)}, u32[]{:S(2)}) %copy-start) | copy-done | bytes 12845080
  97.8 0.0 copy-start.2
  97.8 1.2 %copy-done.2 = bf16[256,1792]{1,0:T(8,128)(2,1)S(1)} copy-done((bf16[256,1792]{1,0:T(8,128)(2,1)S(1)}, bf16[256,1792]{1,0:T(8,128)(2,1)}, u32[]{:S(2)}) %copy-start.2) | copy-done | bytes 917528
  99.0 5.2 %shard_map.67 = (f32[256,1792]{1,0:T(8,128)S(1)}, f32[256,1792]{1,0:T(8,128)S(1)}) custom-call(s32[1]{0:T(128)} %bitcast.index_ref, bf16[256,1792]{1,0:T(8,128)(2,1)S(1)} %copy-done.1, bf16[256,1792]{1,0:T(8,128)(2,1)S(1)} %copy-done.2, bf16[1792,3584]{1,0:T(8,128)(2,1)S(1)} %copy-done), custom_call_target="tpu_custom_call" | custom-call | flops 3288334336 | bytes 11927552 | tf_op jit(solution)/shard_map/pallas_call | solution.py:344
  104.2 0.0 collective-permute-done
  104.2 0.2 add_convert_fusion.1
  104.4 10.5 %collective-permute-done.1 = bf16[256,1792]{1,0:T(8,128)(2,1)S(1)} collective-permute-done((bf16[256,1792]{1,0:T(8,128)(2,1)}, bf16[256,1792]{1,0:T(8,128)(2,1)S(1)}, u32[]{:S(2)}, u32[]{:S(2)}) %collective-permute-start.1) | collective-permute-done | bytes 917536 | tf_op jit(solution)/shard_map/ppermute | solution.py:448
  115.0 0.2 add_convert_fusion
  115.2 1.3 %pad_maximum_fusion = bf16[512,1792]{1,0:T(8,128)(2,1)} fusion(bf16[256,1792]{1,0:T(8,128)(2,1)S(1)} %add_convert_fusion, bf16[256,1792]{1,0:T(8,128)(2,1)S(1)} %add_convert_fusion.1), kind=kLoop, calls=%fused_computation.1 | loop fusion | flops 3670016 | bytes 3670016 | tf_op jit(solution)/shard_map/concatenate | solution.py:451
  (6 shorter events, 0.0 us)
Async XLA Ops:
  65.7 27.5 %copy-start.1 = (bf16[256,1792]{1,0:T(8,128)(2,1)S(1)}, bf16[256,1792]{1,0:T(8,128)(2,1)}, u32[]{:S(2)}) copy-start(bf16[256,1792]{1,0:T(8,128)(2,1)} %get-tuple-element.17.refs_0_) | copy-start | bytes 2752516
  65.7 38.5 %collective-permute-start = (bf16[256,1792]{1,0:T(8,128)(2,1)}, bf16[256,1792]{1,0:T(8,128)(2,1)S(1)}, u32[]{:S(2)}, u32[]{:S(2)}) collective-permute-start(bf16[256,1792]{1,0:T(8,128)(2,1)} %get-tuple-element.20), channel_id=1, source_target_pairs={{0,1},{1,0},{2,3},{3,2},{4,5},{5,4},{6,7},{7,6},{8,9},{9,8},{10,11... | collective-permute-start | bytes 2752520 | tf_op jit(solution)/shard_map/ppermute | solution.py:448
  92.6 22.4 %collective-permute-start.1 = (bf16[256,1792]{1,0:T(8,128)(2,1)}, bf16[256,1792]{1,0:T(8,128)(2,1)S(1)}, u32[]{:S(2)}, u32[]{:S(2)}) collective-permute-start(bf16[256,1792]{1,0:T(8,128)(2,1)} %get-tuple-element.22), channel_id=1, source_target_pairs={{0,1},{1,0},{2,3},{3,2},{4,5},{5,4},{6,7},{7,6},{8,9},{9,8},{10,11... | collective-permute-start | bytes 2752520 | tf_op jit(solution)/shard_map/ppermute | solution.py:448
  93.2 4.7 %copy-start = (bf16[1792,3584]{1,0:T(8,128)(2,1)S(1)}, bf16[1792,3584]{1,0:T(8,128)(2,1)}, u32[]{:S(2)}) copy-start(bf16[1792,3584]{1,0:T(8,128)(2,1)} %refs_2_.1) | copy-start | bytes 38535172
  97.8 1.2 %copy-start.2 = (bf16[256,1792]{1,0:T(8,128)(2,1)S(1)}, bf16[256,1792]{1,0:T(8,128)(2,1)}, u32[]{:S(2)}) copy-start(bf16[256,1792]{1,0:T(8,128)(2,1)} %get-tuple-element.18.refs_1_) | copy-start | bytes 2752516
